TPU v7x, 256 devices: a whole 4x4x8 slice. The times are simulated.
256 devices in a mesh: tm: 16 (over y, x_hi, core), space: 16 (over z, x_lo).
Axes of the slice: x: 4 (x_hi: 2, x_lo: 2; x = x_hi * 2 + x_lo), y: 4, z: 8, core: 2. Of those that a mesh axis runs over, the one named last changes fastest.
Arguments:
- current: bfloat16 [32, 64, 256, 128], P('tm', None, 'space'), may hold values from -6 to 6
- contexts: bfloat16 [32, 64, 256, 128], P('tm', None, 'space'), may hold values from -6 to 6
- cotangent: bfloat16 [32, 64, 256, 128], P('tm', None, 'space'), may hold values from -6 to 6
- level_table: int32 [32], P('tm'), may hold values from 1 to 2, as said below
- ref_table: int32 [32, 2], P('tm'), may hold values from -1 to 32, as said below
- w_first: bfloat16 [2, 9, 64, 192], replicated, may hold values from -0.25 to 0.25
- w_rest: bfloat16 [2, 4, 9, 64, 64], replicated, may hold values from -0.375 to 0.375
Outputs:
- output: bfloat16 [32, 64, 256, 128], P('tm', None, 'space')
- ref_grad: float32 [32, 64, 256, 128], P('tm', None, 'space')
Inputs may be any that keep to these rules, and one draw needn't show every extreme that they name: level_table[f] is 1 for the frames f with (f + p) % 4 == 0 and 2 for the others, p one drawn phase of 0 to 3. ref_table[f, 0] = f - d and ref_table[f, 1] = f + d with d = 4 for level 1 and d = 2 for level 2, without wrapping; a reference before the window is stored as -1 and one after it as 32.
All inputs are finite; a program needn't handle non-finite values.
Results may differ from a plain program's by a relative error of at most 0.02.
Values may be sent and summed in bfloat16 or wider, within the bound.
A program may use at most 64 MiB of HBM per device.

v0:
```python
import jax
import jax.numpy as jnp
from jax import lax
from jax.experimental import pallas as pl
from jax.experimental.pallas import tpu as pltpu
from jax.sharding import PartitionSpec as P

MESH = pl.DeviceIdType.MESH
F32 = jnp.float32
BF = jnp.bfloat16
C = 64
W = 128
H = 16
ODD, EVEN = 0, 1


def lanes(start, count):
    return slice(start * W, (start + count) * W)


def shifted(a):
    n = a.shape[1]
    lane = lax.broadcasted_iota(jnp.int32, a.shape, 1) & (W - 1)
    left = jnp.where(lane == 0, 0.0, pltpu.roll(a, 1, 1))
    right = jnp.where(lane == W - 1, 0.0, pltpu.roll(a, n - 1, 1))
    return left, right


def put(ref, where, a, flip=False, base=0):
    left, right = shifted(a)
    first, last = (right, left) if flip else (left, right)
    ref[base : base + C, where] = first.astype(BF)
    ref[base + C : base + 2 * C, where] = a.astype(BF)
    ref[base + 2 * C : base + 3 * C, where] = last.astype(BF)


def conv(weights, stack, flip=False, out_channels=C):
    t = jnp.dot(weights, stack, preferred_element_type=F32)
    rows = stack.shape[1] // W - 2
    o = out_channels
    first, last = (t[2 * o : 3 * o], t[0:o]) if flip else (t[0:o], t[2 * o : 3 * o])
    return first[:, lanes(0, rows)] + t[o : 2 * o, lanes(1, rows)] + last[:, lanes(2, rows)]


def body(
    nt, ns, level, cur, ctx, cot, wf, wr, out, rg,
    flat, tctx, flag_s, flag_r, mctx, sel_o, sel_l, x_o, x_l, m_l, tcur, tcot,
    stack, stack_c, stack_g, stack_3, p1_cur, g4, p1, d1, d2, d3, d4, outs,
    h1_s, h1_r, h3_s, h3_r, om_s, om_r, ox_s, ox_r, em_s, em_r, ex_s, ex_r, ey_r,
    w_fwd, w_bwd, w_ctx, w_back, ssem, rsem,
):
    tm = lax.axis_index("tm")
    sp = lax.axis_index("space")
    core = lax.rem(tm, 2)
    mate = tm + 1 - 2 * core
    cross = tm - 1 + 2 * core
    cross_ok = (cross >= 0) & (cross < nt)
    up_ok = sp < ns - 1
    dn_ok = sp > 0
    always = tm >= 0
    sent = []

    def link(i, src, dst, device):
        return pltpu.make_async_remote_copy(
            src_ref=src, dst_ref=dst, send_sem=ssem.at[i], recv_sem=rsem.at[i],
            device_id=device, device_id_type=MESH,
        )

    def send(i, src, dst, device, ok):
        @pl.when(ok)
        def _():
            link(i, src, dst, device).start()

        sent.append((i, src, dst, device, ok))

    def arrive(i, src, dst, ok):
        @pl.when(ok)
        def _():
            link(i, src, dst, (tm, sp)).wait_recv()

    partners = []
    for who, who_ok in ((mate, always), (cross, cross_ok)):
        partners.append((who, sp, who_ok))
        partners.append((who, sp + 1, who_ok & up_ok))
        partners.append((who, sp - 1, who_ok & dn_ok))
    partners.append((tm, sp + 1, up_ok))
    partners.append((tm, sp - 1, dn_ok))
    barrier = pltpu.get_barrier_semaphore()
    for a, b, ok in partners:
        @pl.when(ok)
        def _():
            pl.semaphore_signal(barrier, inc=1, device_id=(a, b), device_id_type=MESH)

    def rows_first(src, i, dst, row0):
        flat[...] = src[i].astype(F32).reshape(C * H, W)
        for r in range(H):
            dst[i, :, lanes(row0 + r, 1)] = flat[pl.ds(r, C, stride=H), :].astype(BF)

    has_l0 = level[0] == 1
    has_l1 = level[1] == 1
    has_l = has_l0 | has_l1
    flag_s[...] = jnp.full((16, W), jnp.where(has_l0, 1.0, 0.0), F32).astype(BF)
    for i in range(2):
        rows_first(ctx, i, tctx, 0)
    spans = 1 + up_ok.astype(jnp.int32) + dn_ok.astype(jnp.int32)
    pl.semaphore_wait(barrier, spans * (2 + cross_ok.astype(jnp.int32)) - 1)

    send(0, flag_s, flag_r, (mate, sp), always)
    send(1, tctx, mctx.at[:, :, lanes(1, H)], (mate, sp), always)
    send(2, tctx.at[:, :, lanes(H - 1, 1)], mctx.at[:, :, lanes(0, 1)], (mate, sp + 1), up_ok)
    send(3, tctx.at[:, :, lanes(0, 1)], mctx.at[:, :, lanes(H + 1, 1)], (mate, sp - 1), dn_ok)
    for i in range(2):
        rows_first(cur, i, tcur, 1)
    send(4, tcur.at[:, :, lanes(H, 1)], tcur.at[:, :, lanes(0, 1)], (tm, sp + 1), up_ok)
    send(5, tcur.at[:, :, lanes(1, 1)], tcur.at[:, :, lanes(H + 1, 1)], (tm, sp - 1), dn_ok)

    arrive(0, flag_s, flag_r, always)
    mate_l0 = jnp.broadcast_to(flag_r[0:1, :].astype(F32), (C, W))
    even0 = jnp.maximum(mate_l0, jnp.where(has_l0, 1.0, 0.0))
    even_first = even0 > 0.5

    def wide(n):
        return jnp.concatenate([even0] * n, axis=1) > 0.5

    def pick(which, zero, one):
        zero, one = zero.astype(F32), one.astype(F32)
        mask = wide(zero.shape[1] // W)
        return jnp.where(mask, zero, one) if which == EVEN else jnp.where(mask, one, zero)

    sel_o[...] = pick(ODD, tctx[0], tctx[1]).astype(BF)
    send(6, sel_o, x_o.at[:, lanes(1, H)], (cross, sp), cross_ok)
    send(7, sel_o.at[:, lanes(H - 1, 1)], x_o.at[:, lanes(0, 1)], (cross, sp + 1), cross_ok & up_ok)
    send(8, sel_o.at[:, lanes(0, 1)], x_o.at[:, lanes(H + 1, 1)], (cross, sp - 1), cross_ok & dn_ok)
    arrive(1, tctx, mctx.at[:, :, lanes(1, H)], always)
    mate_even = pick(EVEN, mctx[0, :, lanes(1, H)], mctx[1, :, lanes(1, H)])
    sel_l[...] = jnp.where(has_l, pick(EVEN, tctx[0], tctx[1]), mate_even).astype(BF)
    send(9, sel_l, x_l.at[:, lanes(1, H)], (cross, sp), cross_ok)
    send(10, sel_l.at[:, lanes(H - 1, 1)], x_l.at[:, lanes(0, 1)], (cross, sp + 1), cross_ok & up_ok)
    send(11, sel_l.at[:, lanes(0, 1)], x_l.at[:, lanes(H + 1, 1)], (cross, sp - 1), cross_ok & dn_ok)

    for i in range(2):
        rows_first(cot, i, tcot, 2)
    send(12, tcot.at[:, :, lanes(H, 2)], tcot.at[:, :, lanes(0, 2)], (tm, sp + 1), up_ok)
    send(13, tcot.at[:, :, lanes(2, 2)], tcot.at[:, :, lanes(H + 2, 2)], (tm, sp - 1), dn_ok)

    def clear(ok, ref, where, lead):
        @pl.when(jnp.logical_not(ok))
        def _():
            for c in range(lead):
                view = ref.at[c] if lead > 1 else ref
                n = where.stop - where.start
                view[:, where] = jnp.zeros((C, n), BF)

    clear(dn_ok, tcur, lanes(0, 1), 2)
    clear(up_ok, tcur, lanes(H + 1, 1), 2)
    clear(dn_ok, tcot, lanes(0, 2), 2)
    clear(up_ok, tcot, lanes(H + 2, 2), 2)
    clear(dn_ok, mctx, lanes(0, 1), 2)
    clear(up_ok, mctx, lanes(H + 1, 1), 2)
    for ref in (x_o, x_l):
        clear(cross_ok, ref, lanes(1, H), 1)
        clear(cross_ok & dn_ok, ref, lanes(0, 1), 1)
        clear(cross_ok & up_ok, ref, lanes(H + 1, 1), 1)
    mate_cross = tm + 2 - 4 * core
    mate_cross_ok = (mate_cross >= 0) & (mate_cross < nt)
    clear(mate_cross_ok, m_l, lanes(0, H + 2), 1)
    for c in range(2):
        clear(dn_ok, h1_r.at[c, 0], lanes(0, 4), 1)
        clear(up_ok, h1_r.at[c, 1], lanes(0, 4), 1)
        clear(dn_ok, h3_r.at[c, 0], lanes(0, 3), 1)
        clear(up_ok, h3_r.at[c, 1], lanes(0, 3), 1)
    clear(cross_ok, ox_r, lanes(0, H), 1)
    clear(cross_ok, ex_r, lanes(0, H), 1)
    clear(mate_cross_ok, ey_r, lanes(0, H), 1)

    eye_r = lax.broadcasted_iota(jnp.int32, (3 * C, 3 * C), 0)
    eye_c = lax.broadcasted_iota(jnp.int32, (3 * C, 3 * C), 1)
    eye = jnp.where(eye_r == eye_c, 1.0, 0.0).astype(BF)

    def turned(m):
        return lax.dot_general(
            eye[: m.shape[1], : m.shape[1]], m, (((1,), (1,)), ((), ())), preferred_element_type=F32
        ).astype(BF)

    for c in (ODD, EVEN):
        def first_tap(t):
            if c == ODD:
                return wf[1, t]
            return jnp.where(has_l, wf[0, t].astype(F32), wf[1, t].astype(F32)).astype(BF)

        def rest_tap(k, t):
            if c == ODD:
                return wr[1, k, t]
            return jnp.where(has_l, wr[0, k, t].astype(F32), wr[1, k, t].astype(F32)).astype(BF)

        taps = [first_tap(t) for t in range(9)]
        for g in range(3):
            part = [tap[:, g * C : (g + 1) * C] for tap in taps]
            for a in range(3):
                rows = jnp.concatenate(part[3 * a : 3 * a + 3], axis=1)
                if g == 0:
                    w_fwd[c, 0, a * C : (a + 1) * C, :] = rows
                else:
                    w_ctx[c, a * C : (a + 1) * C, (g - 1) * 3 * C : g * 3 * C] = rows
        both = [tap[:, C:] for tap in taps]
        for a in range(3):
            m = jnp.concatenate([both[3 * a + b] for b in range(3)], axis=0)
            w_back[c, a * 2 * C : (a + 1) * 2 * C, :] = turned(m)
        for k in range(4):
            part = [rest_tap(k, t) for t in range(9)]
            for a in range(3):
                w_fwd[c, k + 1, a * C : (a + 1) * C, :] = jnp.concatenate(part[3 * a : 3 * a + 3], axis=1)
                m = jnp.concatenate([part[3 * a + b] for b in range(3)], axis=0)
                w_bwd[c, k, a * C : (a + 1) * C, :] = turned(m)

    arrive(4, tcur.at[:, :, lanes(H, 1)], tcur.at[:, :, lanes(0, 1)], dn_ok)
    arrive(5, tcur.at[:, :, lanes(1, 1)], tcur.at[:, :, lanes(H + 1, 1)], up_ok)
    for c in (ODD, EVEN):
        put(stack, lanes(0, H + 2), pick(c, tcur[0], tcur[1]))
        p1_cur[c] = conv(w_fwd[c, 0], stack[:, lanes(0, H + 2)])
    arrive(12, tcot.at[:, :, lanes(H, 2)], tcot.at[:, :, lanes(0, 2)], dn_ok)
    arrive(13, tcot.at[:, :, lanes(2, 2)], tcot.at[:, :, lanes(H + 2, 2)], up_ok)
    for c in (ODD, EVEN):
        put(stack_g, lanes(0, H + 4), pick(c, tcot[0], tcot[1]), flip=True)
        g4[c] = conv(w_bwd[c, 3], stack_g[:, lanes(0, H + 4)], flip=True)

    arrive(2, tctx.at[:, :, lanes(H - 1, 1)], mctx.at[:, :, lanes(0, 1)], dn_ok)
    arrive(3, tctx.at[:, :, lanes(0, 1)], mctx.at[:, :, lanes(H + 1, 1)], up_ok)
    first_core = core == 0

    def layer_one(c, outer, inner):
        put(stack_c, lanes(0, H + 2), jnp.where(first_core, outer, inner))
        put(stack_c, lanes(0, H + 2), jnp.where(first_core, inner, outer), base=3 * C)
        pre = p1_cur[c] + conv(w_ctx[c], stack_c[...])
        p1[c, :, lanes(4, H)] = pre
        h1_s[c, 0] = pre[:, lanes(H - 4, 4)].astype(BF)
        h1_s[c, 1] = pre[:, lanes(0, 4)].astype(BF)
        send(14 + 2 * c, h1_s.at[c, 0], h1_r.at[c, 0], (tm, sp + 1), up_ok)
        send(15 + 2 * c, h1_s.at[c, 1], h1_r.at[c, 1], (tm, sp - 1), dn_ok)

    def activate(pre, halo):
        sigma = 1.0 / (1.0 + jnp.exp(-pre))
        act = pre * sigma
        slope = sigma * (1.0 + pre * (1.0 - sigma))
        row = (lax.broadcasted_iota(jnp.int32, pre.shape, 1) >> 7) + (sp * H - halo)
        inside = (row >= 0) & (row < ns * H)
        return jnp.where(inside, act, 0.0), jnp.where(inside, slope, 0.0)

    def forward(c):
        arrive(14 + 2 * c, h1_s.at[c, 0], h1_r.at[c, 0], dn_ok)
        arrive(15 + 2 * c, h1_s.at[c, 1], h1_r.at[c, 1], up_ok)
        p1[c, :, lanes(0, 4)] = h1_r[c, 0].astype(F32)
        p1[c, :, lanes(H + 4, 4)] = h1_r[c, 1].astype(F32)
        act, slope = activate(p1[c], 4)
        d1[c] = slope[:, lanes(3, H + 2)]
        put(stack, lanes(0, 24), act)
        act, slope = activate(conv(w_fwd[c, 1], stack[...]), 3)
        d2[c] = slope[:, lanes(1, H + 4)]
        put(stack, lanes(0, 22), act)
        act, slope = activate(conv(w_fwd[c, 2], stack[:, lanes(0, 22)]), 2)
        d3[c] = slope[:, lanes(2, H)]
        put(stack, lanes(0, 20), act)
        act, slope = activate(conv(w_fwd[c, 3], stack[:, lanes(0, 20)]), 1)
        put(stack_g, lanes(0, 18), g4[c] * slope, flip=True)
        s3 = conv(w_bwd[c, 2], stack_g[:, lanes(0, 18)], flip=True) * d3[c]
        h3_s[c, 0] = s3[:, lanes(H - 3, 3)].astype(BF)
        h3_s[c, 1] = s3[:, lanes(0, 3)].astype(BF)
        send(18 + 2 * c, h3_s.at[c, 0], h3_r.at[c, 0], (tm, sp + 1), up_ok)
        send(19 + 2 * c, h3_s.at[c, 1], h3_r.at[c, 1], (tm, sp - 1), dn_ok)
        put(stack_3.at[c], lanes(3, H), s3, flip=True)
        put(stack, lanes(0, 18), act)
        own = pick(c, tcur[0, :, lanes(1, H)], tcur[1, :, lanes(1, H)])
        outs[c] = own + conv(w_fwd[c, 4], stack[:, lanes(0, 18)])

    def backward(c):
        arrive(18 + 2 * c, h3_s.at[c, 0], h3_r.at[c, 0], dn_ok)
        arrive(19 + 2 * c, h3_s.at[c, 1], h3_r.at[c, 1], up_ok)
        put(stack_3.at[c], lanes(0, 3), h3_r[c, 0].astype(F32), flip=True)
        put(stack_3.at[c], lanes(H + 3, 3), h3_r[c, 1].astype(F32), flip=True)
        s2 = conv(w_bwd[c, 1], stack_3[c], flip=True) * d2[c]
        put(stack_g, lanes(0, 20), s2, flip=True)
        s1 = conv(w_bwd[c, 0], stack_g[:, lanes(0, 20)], flip=True) * d1[c]
        put(stack_g, lanes(0, 18), s1, flip=True)
        grads = conv(w_back[c], stack_g[:, lanes(0, 18)], flip=True, out_channels=2 * C)
        behind, ahead = grads[:C], grads[C:]
        return jnp.where(first_core, behind, ahead), jnp.where(first_core, ahead, behind)

    arrive(6, sel_o, x_o.at[:, lanes(1, H)], cross_ok)
    arrive(7, sel_o.at[:, lanes(H - 1, 1)], x_o.at[:, lanes(0, 1)], cross_ok & dn_ok)
    arrive(8, sel_o.at[:, lanes(0, 1)], x_o.at[:, lanes(H + 1, 1)], cross_ok & up_ok)
    layer_one(ODD, x_o[...].astype(F32), pick(ODD, mctx[0], mctx[1]))
    arrive(9, sel_l, x_l.at[:, lanes(1, H)], cross_ok)
    arrive(10, sel_l.at[:, lanes(H - 1, 1)], x_l.at[:, lanes(0, 1)], cross_ok & dn_ok)
    arrive(11, sel_l.at[:, lanes(0, 1)], x_l.at[:, lanes(H + 1, 1)], cross_ok & up_ok)
    send(22, x_l, m_l, (mate, sp), cross_ok)
    forward(ODD)
    arrive(22, x_l, m_l, mate_cross_ok)
    inner = jnp.where(has_l, m_l[...].astype(F32), pick(EVEN, mctx[0], mctx[1]))
    layer_one(EVEN, x_l[...].astype(F32), inner)
    outer_g, inner_g = backward(ODD)
    ox_s[...] = outer_g.astype(BF)
    send(23, ox_s, ox_r, (cross, sp), cross_ok)
    om_s[...] = inner_g.astype(BF)
    send(24, om_s, om_r, (mate, sp), always)
    forward(EVEN)
    outer_g, inner_g = backward(EVEN)
    em_s[...] = inner_g.astype(BF)
    send(25, em_s, em_r, (mate, sp), always)
    arrive(25, em_s, em_r, always)
    from_mate = em_r[...].astype(F32)
    ex_s[...] = (outer_g + jnp.where(has_l, 0.0, from_mate)).astype(BF)
    send(26, ex_s, ex_r, (cross, sp), cross_ok)
    mask = wide(H)
    out[0] = jnp.where(mask, outs[EVEN], outs[ODD]).astype(BF)
    out[1] = jnp.where(mask, outs[ODD], outs[EVEN]).astype(BF)
    arrive(23, ox_s, ox_r, cross_ok)
    arrive(24, om_s, om_r, always)
    odd_g = ox_r[...].astype(F32) + om_r[...].astype(F32)
    arrive(26, ex_s, ex_r, cross_ok)
    send(27, ex_r, ey_r, (mate, sp), cross_ok)
    arrive(27, ex_r, ey_r, mate_cross_ok)
    even_g = ex_r[...].astype(F32) + ey_r[...].astype(F32) + from_mate
    even_g = jnp.where(has_l, even_g, 0.0)
    rg[0] = jnp.where(mask, even_g, odd_g)
    rg[1] = jnp.where(mask, odd_g, even_g)
    for i, src, dst, device, ok in sent:
        @pl.when(ok)
        def _():
            link(i, src, dst, device).wait_send()


def solution(mesh):
    nt, ns = mesh.shape["tm"], mesh.shape["space"]

    def on_device(current, contexts, cotangent, level_table, ref_table, w_first, w_rest):
        vmem = pl.BlockSpec(memory_space=pltpu.VMEM)

        def bf(*shape):
            return pltpu.VMEM(shape, BF)

        def f32(*shape):
            return pltpu.VMEM(shape, F32)

        slab = H * W
        halo = (H + 2) * W
        scratch = [
            f32(C * H, W), bf(2, C, slab), bf(16, W), bf(16, W), bf(2, C, halo), bf(C, slab), bf(C, slab),
            bf(C, halo), bf(C, halo), bf(C, halo), bf(2, C, halo), bf(2, C, (H + 4) * W),
            bf(3 * C, 24 * W), bf(6 * C, halo), bf(3 * C, 20 * W), bf(2, 3 * C, 22 * W),
            f32(2, C, slab), f32(2, C, halo), f32(2, C, 24 * W),
            f32(2, C, halo), f32(2, C, (H + 4) * W), f32(2, C, slab), f32(2, C, halo), f32(2, C, slab),
            bf(2, 2, C, 4 * W), bf(2, 2, C, 4 * W), bf(2, 2, C, 3 * W), bf(2, 2, C, 3 * W),
            bf(C, slab), bf(C, slab), bf(C, slab), bf(C, slab),
            bf(C, slab), bf(C, slab), bf(C, slab), bf(C, slab), bf(C, slab),
            bf(2, 5, 3 * C, 3 * C), bf(2, 4, 3 * C, 3 * C), bf(2, 3 * C, 6 * C), bf(2, 6 * C, 3 * C),
            pltpu.SemaphoreType.DMA((28,)), pltpu.SemaphoreType.DMA((28,)),
        ]

        def kernel(*refs):
            body(nt, ns, *refs)

        out, rg = pl.pallas_call(
            kernel,
            out_shape=(
                jax.ShapeDtypeStruct((2, C, slab), BF),
                jax.ShapeDtypeStruct((2, C, slab), F32),
            ),
            in_specs=[pl.BlockSpec(memory_space=pltpu.SMEM)] + [vmem] * 5,
            out_specs=(vmem, vmem),
            scratch_shapes=scratch,
            compiler_params=pltpu.CompilerParams(
                collective_id=0, has_side_effects=True, vmem_limit_bytes=56 << 20
            ),
            name="coding",
        )(level_table, current, contexts, cotangent, w_first, w_rest)
        return out.reshape(2, C, H, W), rg.reshape(2, C, H, W)

    frames = P("tm", None, "space", None)
    return jax.shard_map(
        on_device,
        mesh=mesh,
        in_specs=(frames, frames, frames, P("tm"), P("tm", None), P(), P()),
        out_specs=(frames, frames),
        check_vma=False,
    )
```

profile of v0, /device:TPU:169, one launch (start us, length us, event | category | flops | bytes accessed | tf_op | source)
XLA Modules:
  0.0 67.8 jit_solution(2828136920477333739)
XLA Ops:
  0.6 63.9 %coding.1 = (bf16[2,64,2048]{2,1,0:T(8,128)(2,1)}, f32[2,64,2048]{2,1,0:T(8,128)}) custom-call(s32[2]{0:T(128)} %refs_0_.1, bf16[2,64,16,128]{3,2,1,0:T(8,128)(2,1)} %refs_1_.1, bf16[2,64,16,128]{3,2,1,0:T(8,128)(2,1)} %refs_2_.1, bf16[2,64,16,128]{3,2,1,0:T(8,128)(2,1)} %refs_3_.1, bf16[2,9,64,192]{3,2,1,0:T(8,128)(2,1)} %refs_4_.1, ...), custom_call_target="tpu_custom_call" | custom-call | tf_op jit(solution)/shard_map/coding/pallas_call | solution.py:362
  64.6 0.0 copy-start
  64.6 2.0 %copy.8 = bf16[16,8,16,128]{3,2,1,0:T(8,128)(2,1)} copy(bf16[16,8,16,128]{3,1,2,0:T(8,128)(2,1)} %bitcast.11) | data formatting | bytes 1048576
  66.6 0.0 copy-done
  66.6 1.2 %copy.9 = f32[16,8,16,128]{3,2,1,0:T(8,128)} copy(f32[16,8,16,128]{3,1,2,0:T(8,128)S(1)} %bitcast.9) | data formatting | bytes 2097152
Async XLA Ops:
  64.6 2.0 %copy-start = (f32[2,64,2048]{2,1,0:T(8,128)S(1)}, f32[2,64,2048]{2,1,0:T(8,128)}, u32[]{:S(2)}) copy-start(f32[2,64,2048]{2,1,0:T(8,128)} %get-tuple-element.5) | copy-start | bytes 3145732
where the time goes:
time: 67.9 us; the launch traced here: 67.8 us
  Pallas kernels  63.9 us (94%)
  local copies, waits for them, and re-layouts  3.2 us (5%)
    pallas_call x1, Pallas kernels, on_device(): pl.pallas_call(kernel, out_shape=(jax.ShapeDtypeStruct((2, C, slab), BF),...  63.9 us
    unnamed x4, local copies, waits for them, and re-layouts  3.2 us

commit v1 on v0

v1 whole, which is shorter than its diff:
```python
import jax
import jax.numpy as jnp
from jax import lax
from jax.experimental import pallas as pl
from jax.experimental.pallas import tpu as pltpu
from jax.sharding import PartitionSpec as P

MESH = pl.DeviceIdType.MESH
F32 = jnp.float32
BF = jnp.bfloat16
C = 64
W = 128
H = 16
ODD, EVEN = 0, 1


def lanes(start, count):
    return slice(start * W, (start + count) * W)


def shifted(a):
    n = a.shape[1]
    lane = lax.broadcasted_iota(jnp.int32, a.shape, 1) & (W - 1)
    left = jnp.where(lane == 0, 0.0, pltpu.roll(a, 1, 1))
    right = jnp.where(lane == W - 1, 0.0, pltpu.roll(a, n - 1, 1))
    return left, right


def put(ref, where, a, flip=False, base=0):
    left, right = shifted(a)
    first, last = (right, left) if flip else (left, right)
    ref[base : base + C, where] = first.astype(BF)
    ref[base + C : base + 2 * C, where] = a.astype(BF)
    ref[base + 2 * C : base + 3 * C, where] = last.astype(BF)


def conv(weights, stack, flip=False, out_channels=C):
    t = jnp.dot(weights, stack, preferred_element_type=F32)
    rows = stack.shape[1] // W - 2
    o = out_channels
    first, last = (t[2 * o : 3 * o], t[0:o]) if flip else (t[0:o], t[2 * o : 3 * o])
    return first[:, lanes(0, rows)] + t[o : 2 * o, lanes(1, rows)] + last[:, lanes(2, rows)]


def body(
    nt, ns, level, cur, ctx, cot, wf, wr, out, rg,
    flat, tctx, flag_s, flag_r, mctx, sel_o, sel_l, x_o, x_l, m_l, tcur, tcot, ccot,
    stack, stack_c, stack_g, stack_3, stack_4, p1_cur, g4_o, g4_e, p1_o, p1_e, d1, d2, d3_o, d3_e, outs,
    h1o_s, h1o_r, h1e_s, h1e_r, h3_s, h3_r, om_s, om_r, ox_s, ox_r, em_s, em_r, ex_s, ex_r, ey_r,
    w_fwd, w_bwd, w_ctx, w_back, ssem, rsem,
):
    tm = lax.axis_index("tm")
    sp = lax.axis_index("space")
    core = lax.rem(tm, 2)
    mate = tm + 1 - 2 * core
    cross = tm - 1 + 2 * core
    cross_ok = (cross >= 0) & (cross < nt)
    up_ok = sp < ns - 1
    dn_ok = sp > 0
    always = tm >= 0
    sent = {}
    left = set()
    g4, p1, d3, h1_s, h1_r = (g4_o, g4_e), (p1_o, p1_e), (d3_o, d3_e), (h1o_s, h1e_s), (h1o_r, h1e_r)

    def link(i, src, dst, device):
        return pltpu.make_async_remote_copy(
            src_ref=src, dst_ref=dst, send_sem=ssem.at[i], recv_sem=rsem.at[i],
            device_id=device, device_id_type=MESH,
        )

    def send(i, src, dst, device, ok, from_ok):
        @pl.when(ok)
        def _():
            link(i, src, dst, device).start()

        sent[i] = (src, dst, device, ok, from_ok)

    def arrive(*which):
        for i in which:
            src, dst, _, _, ok = sent[i]

            @pl.when(ok)
            def _():
                link(i, src, dst, (tm, sp)).wait_recv()

    def gone(*which):
        for i in which:
            src, dst, device, ok, _ = sent[i]
            left.add(i)

            @pl.when(ok)
            def _():
                link(i, src, dst, device).wait_send()

    partners = []
    for who, who_ok in ((mate, always), (cross, cross_ok)):
        partners.append((who, sp, who_ok))
        partners.append((who, sp + 1, who_ok & up_ok))
        partners.append((who, sp - 1, who_ok & dn_ok))
    partners.append((tm, sp + 1, up_ok))
    partners.append((tm, sp - 1, dn_ok))
    barrier = pltpu.get_barrier_semaphore()
    for a, b, ok in partners:
        @pl.when(ok)
        def _():
            pl.semaphore_signal(barrier, inc=1, device_id=(a, b), device_id_type=MESH)

    def rows_first(src, i, dst, row0):
        flat[...] = src[i].astype(F32).reshape(C * H, W)
        for r in range(H):
            dst[i, :, lanes(row0 + r, 1)] = flat[pl.ds(r, C, stride=H), :].astype(BF)

    has_l0 = level[0] == 1
    has_l1 = level[1] == 1
    has_l = has_l0 | has_l1
    flag_s[...] = jnp.full((16, W), jnp.where(has_l0, 1.0, 0.0), F32).astype(BF)
    for i in range(2):
        rows_first(ctx, i, tctx, 0)
    spans = 1 + up_ok.astype(jnp.int32) + dn_ok.astype(jnp.int32)
    pl.semaphore_wait(barrier, spans * (2 + cross_ok.astype(jnp.int32)) - 1)

    send(0, flag_s, flag_r, (mate, sp), always, always)
    send(1, tctx, mctx.at[:, :, lanes(1, H)], (mate, sp), always, always)
    send(2, tctx.at[:, :, lanes(H - 1, 1)], mctx.at[:, :, lanes(0, 1)], (mate, sp + 1), up_ok, dn_ok)
    send(3, tctx.at[:, :, lanes(0, 1)], mctx.at[:, :, lanes(H + 1, 1)], (mate, sp - 1), dn_ok, up_ok)
    for i in range(2):
        rows_first(cur, i, tcur, 1)
    send(4, tcur.at[:, :, lanes(H, 1)], tcur.at[:, :, lanes(0, 1)], (tm, sp + 1), up_ok, dn_ok)
    send(5, tcur.at[:, :, lanes(1, 1)], tcur.at[:, :, lanes(H + 1, 1)], (tm, sp - 1), dn_ok, up_ok)

    arrive(0)
    mate_l0 = jnp.broadcast_to(flag_r[0:1, :].astype(F32), (C, W))
    even0 = jnp.maximum(mate_l0, jnp.where(has_l0, 1.0, 0.0))

    def wide(n):
        return jnp.concatenate([even0] * n, axis=1) > 0.5

    def pick(which, zero, one):
        zero, one = zero.astype(F32), one.astype(F32)
        mask = wide(zero.shape[1] // W)
        return jnp.where(mask, zero, one) if which == EVEN else jnp.where(mask, one, zero)

    arrive(1)
    mate_even = pick(EVEN, mctx[0, :, lanes(1, H)], mctx[1, :, lanes(1, H)])
    sel_l[...] = jnp.where(has_l, pick(EVEN, tctx[0], tctx[1]), mate_even).astype(BF)
    send(9, sel_l, x_l.at[:, lanes(1, H)], (cross, sp), cross_ok, cross_ok)
    send(10, sel_l.at[:, lanes(H - 1, 1)], x_l.at[:, lanes(0, 1)], (cross, sp + 1), cross_ok & up_ok, cross_ok & dn_ok)
    send(11, sel_l.at[:, lanes(0, 1)], x_l.at[:, lanes(H + 1, 1)], (cross, sp - 1), cross_ok & dn_ok, cross_ok & up_ok)
    sel_o[...] = pick(ODD, tctx[0], tctx[1]).astype(BF)

    for i in range(2):
        rows_first(cot, i, tcot, 0)
    for c, halo in ((ODD, 5), (EVEN, 2)):
        ccot[c, :, lanes(5, H)] = pick(c, tcot[0], tcot[1]).astype(BF)
        top, bottom = lanes(5 - halo, halo), lanes(H + 5, halo)
        send(12 + 8 * c, ccot.at[c, :, lanes(H + 5 - halo, halo)], ccot.at[c, :, top], (tm, sp + 1), up_ok, dn_ok)
        send(13 + 8 * c, ccot.at[c, :, lanes(5, halo)], ccot.at[c, :, bottom], (tm, sp - 1), dn_ok, up_ok)

    def clear(ok, ref, where, lead):
        @pl.when(jnp.logical_not(ok))
        def _():
            for c in range(lead):
                view = ref.at[c] if lead > 1 else ref
                n = where.stop - where.start
                view[:, where] = jnp.zeros((C, n), BF)

    clear(dn_ok, tcur, lanes(0, 1), 2)
    clear(up_ok, tcur, lanes(H + 1, 1), 2)
    clear(dn_ok, ccot, lanes(0, 5), 2)
    clear(up_ok, ccot, lanes(H + 5, 5), 2)
    clear(dn_ok, mctx, lanes(0, 1), 2)
    clear(up_ok, mctx, lanes(H + 1, 1), 2)
    for ref in (x_o, x_l):
        clear(cross_ok, ref, lanes(1, H), 1)
        clear(cross_ok & dn_ok, ref, lanes(0, 1), 1)
        clear(cross_ok & up_ok, ref, lanes(H + 1, 1), 1)
    mate_cross = tm + 2 - 4 * core
    mate_cross_ok = (mate_cross >= 0) & (mate_cross < nt)
    clear(mate_cross_ok, m_l, lanes(0, H + 2), 1)
    for ref, n in ((h1o_r, 7), (h1e_r, 4), (h3_r, 3)):
        clear(dn_ok, ref.at[0], lanes(0, n), 1)
        clear(up_ok, ref.at[1], lanes(0, n), 1)
    clear(cross_ok, ox_r, lanes(0, H), 1)
    clear(cross_ok, ex_r, lanes(0, H), 1)
    clear(mate_cross_ok, ey_r, lanes(0, H), 1)

    eye_r = lax.broadcasted_iota(jnp.int32, (3 * C, 3 * C), 0)
    eye_c = lax.broadcasted_iota(jnp.int32, (3 * C, 3 * C), 1)
    eye = jnp.where(eye_r == eye_c, 1.0, 0.0).astype(BF)

    def turned(m):
        return lax.dot_general(
            eye[: m.shape[1], : m.shape[1]], m, (((1,), (1,)), ((), ())), preferred_element_type=F32
        ).astype(BF)

    for c in (ODD, EVEN):
        def first_tap(t):
            if c == ODD:
                return wf[1, t]
            return jnp.where(has_l, wf[0, t].astype(F32), wf[1, t].astype(F32)).astype(BF)

        def rest_tap(k, t):
            if c == ODD:
                return wr[1, k, t]
            return jnp.where(has_l, wr[0, k, t].astype(F32), wr[1, k, t].astype(F32)).astype(BF)

        taps = [first_tap(t) for t in range(9)]
        for g in range(3):
            part = [tap[:, g * C : (g + 1) * C] for tap in taps]
            for a in range(3):
                rows = jnp.concatenate(part[3 * a : 3 * a + 3], axis=1)
                if g == 0:
                    w_fwd[c, 0, a * C : (a + 1) * C, :] = rows
                else:
                    w_ctx[c, a * C : (a + 1) * C, (g - 1) * 3 * C : g * 3 * C] = rows
        both = [tap[:, C:] for tap in taps]
        for a in range(3):
            m = jnp.concatenate([both[3 * a + b] for b in range(3)], axis=0)
            w_back[c, a * 2 * C : (a + 1) * 2 * C, :] = turned(m)
        for k in range(4):
            part = [rest_tap(k, t) for t in range(9)]
            for a in range(3):
                w_fwd[c, k + 1, a * C : (a + 1) * C, :] = jnp.concatenate(part[3 * a : 3 * a + 3], axis=1)
                m = jnp.concatenate([part[3 * a + b] for b in range(3)], axis=0)
                w_bwd[c, k, a * C : (a + 1) * C, :] = turned(m)

    gone(9)
    send(6, sel_o, x_o.at[:, lanes(1, H)], (cross, sp), cross_ok, cross_ok)
    send(7, sel_o.at[:, lanes(H - 1, 1)], x_o.at[:, lanes(0, 1)], (cross, sp + 1), cross_ok & up_ok, cross_ok & dn_ok)
    send(8, sel_o.at[:, lanes(0, 1)], x_o.at[:, lanes(H + 1, 1)], (cross, sp - 1), cross_ok & dn_ok, cross_ok & up_ok)

    arrive(4)
    arrive(5)
    for c in (ODD, EVEN):
        put(stack, lanes(0, H + 2), pick(c, tcur[0], tcur[1]))
        p1_cur[c] = conv(w_fwd[c, 0], stack[:, lanes(0, H + 2)])
    for c, halo in ((EVEN, 2), (ODD, 5)):
        arrive(12 + 8 * c, 13 + 8 * c)
        rows = H + 2 * halo
        put(stack_g, lanes(0, rows), ccot[c, :, lanes(5 - halo, rows)].astype(F32), flip=True)
        g4[c][...] = conv(w_bwd[c, 3], stack_g[:, lanes(0, rows)], flip=True)

    arrive(2)
    arrive(3)
    first_core = core == 0
    reach = (7, 4)

    def layer_one(c, outer, inner):
        put(stack_c, lanes(0, H + 2), jnp.where(first_core, outer, inner))
        put(stack_c, lanes(0, H + 2), jnp.where(first_core, inner, outer), base=3 * C)
        pre = p1_cur[c] + conv(w_ctx[c], stack_c[...])
        halo = reach[c]
        p1[c][:, lanes(halo, H)] = pre
        h1_s[c][0] = pre[:, lanes(H - halo, halo)].astype(BF)
        h1_s[c][1] = pre[:, lanes(0, halo)].astype(BF)
        send(14 + 2 * c, h1_s[c].at[0], h1_r[c].at[0], (tm, sp + 1), up_ok, dn_ok)
        send(15 + 2 * c, h1_s[c].at[1], h1_r[c].at[1], (tm, sp - 1), dn_ok, up_ok)

    def activate(pre, halo):
        sigma = 1.0 / (1.0 + jnp.exp(-pre))
        act = pre * sigma
        slope = sigma * (1.0 + pre * (1.0 - sigma))
        row = (lax.broadcasted_iota(jnp.int32, pre.shape, 1) >> 7) + (sp * H - halo)
        inside = (row >= 0) & (row < ns * H)
        return jnp.where(inside, act, 0.0), jnp.where(inside, slope, 0.0)

    def forward(c):
        h = reach[c]
        arrive(14 + 2 * c, 15 + 2 * c)
        p1[c][:, lanes(0, h)] = h1_r[c][0].astype(F32)
        p1[c][:, lanes(H + h, h)] = h1_r[c][1].astype(F32)
        act, slope = activate(p1[c][...], h)
        d1[c] = slope[:, lanes(h - 1, H + 2)]
        for k in (1, 2, 3):
            rows = lanes(0, H + 2 * (h + 1 - k))
            put(stack, rows, act)
            act, slope = activate(conv(w_fwd[c, k], stack[:, rows]), h - k)
            if k == 1:
                d2[c] = slope[:, lanes(h - 3, H + 4)]
            if k == 2:
                d3[c][...] = slope[:, lanes(2, H + 2 * (h - 4))]
        rows = lanes(0, H + 2 * (h - 3))
        put(stack_g, rows, g4[c][...] * slope, flip=True)
        s3 = conv(w_bwd[c, 2], stack_g[:, rows], flip=True) * d3[c][...]
        if c == EVEN:
            h3_s[0] = s3[:, lanes(H - 3, 3)].astype(BF)
            h3_s[1] = s3[:, lanes(0, 3)].astype(BF)
            send(18, h3_s.at[0], h3_r.at[0], (tm, sp + 1), up_ok, dn_ok)
            send(19, h3_s.at[1], h3_r.at[1], (tm, sp - 1), dn_ok, up_ok)
        put(stack_3.at[c], lanes(7 - h, H + 2 * (h - 4)), s3, flip=True)
        put(stack_4.at[c], lanes(0, H + 2), act[:, lanes(h - 4, H + 2)])

    def finish(c):
        own = pick(c, tcur[0, :, lanes(1, H)], tcur[1, :, lanes(1, H)])
        outs[c] = own + conv(w_fwd[c, 4], stack_4[c])

    def backward(c):
        if c == EVEN:
            arrive(18, 19)
            put(stack_3.at[c], lanes(0, 3), h3_r[0].astype(F32), flip=True)
            put(stack_3.at[c], lanes(H + 3, 3), h3_r[1].astype(F32), flip=True)
        s2 = conv(w_bwd[c, 1], stack_3[c], flip=True) * d2[c]
        put(stack_g, lanes(0, 20), s2, flip=True)
        s1 = conv(w_bwd[c, 0], stack_g[:, lanes(0, 20)], flip=True) * d1[c]
        put(stack_g, lanes(0, 18), s1, flip=True)
        grads = conv(w_back[c], stack_g[:, lanes(0, 18)], flip=True, out_channels=2 * C)
        behind, ahead = grads[:C], grads[C:]
        return jnp.where(first_core, behind, ahead), jnp.where(first_core, ahead, behind)

    arrive(9, 10, 11)
    send(22, x_l, m_l, (mate, sp), cross_ok, mate_cross_ok)
    arrive(22)
    inner = jnp.where(has_l, m_l[...].astype(F32), pick(EVEN, mctx[0], mctx[1]))
    layer_one(EVEN, x_l[...].astype(F32), inner)
    forward(EVEN)
    arrive(6, 7, 8)
    layer_one(ODD, x_o[...].astype(F32), pick(ODD, mctx[0], mctx[1]))
    outer_g, inner_g = backward(EVEN)
    em_s[...] = inner_g.astype(BF)
    send(25, em_s, em_r, (mate, sp), always, always)
    finish(EVEN)
    arrive(25)
    from_mate = em_r[...].astype(F32)
    ex_s[...] = (outer_g + jnp.where(has_l, 0.0, from_mate)).astype(BF)
    send(26, ex_s, ex_r, (cross, sp), cross_ok, cross_ok)
    forward(ODD)
    outer_g, inner_g = backward(ODD)
    ox_s[...] = outer_g.astype(BF)
    send(23, ox_s, ox_r, (cross, sp), cross_ok, cross_ok)
    om_s[...] = inner_g.astype(BF)
    send(24, om_s, om_r, (mate, sp), always, always)
    finish(ODD)
    mask = wide(H)
    out[0] = jnp.where(mask, outs[EVEN], outs[ODD]).astype(BF)
    out[1] = jnp.where(mask, outs[ODD], outs[EVEN]).astype(BF)
    arrive(26)
    send(27, ex_r, ey_r, (mate, sp), cross_ok, mate_cross_ok)
    arrive(27)
    even_g = ex_r[...].astype(F32) + ey_r[...].astype(F32) + em_r[...].astype(F32)
    even_g = jnp.where(has_l, even_g, 0.0)
    arrive(24, 23)
    odd_g = ox_r[...].astype(F32) + om_r[...].astype(F32)
    rg[0] = jnp.where(mask, even_g, odd_g)
    rg[1] = jnp.where(mask, odd_g, even_g)
    gone(*(i for i in sent if i not in left))


def solution(mesh):
    nt, ns = mesh.shape["tm"], mesh.shape["space"]

    def on_device(current, contexts, cotangent, level_table, ref_table, w_first, w_rest):
        vmem = pl.BlockSpec(memory_space=pltpu.VMEM)

        def bf(*shape):
            return pltpu.VMEM(shape, BF)

        def f32(*shape):
            return pltpu.VMEM(shape, F32)

        slab = H * W
        halo = (H + 2) * W
        scratch = [
            f32(C * H, W), bf(2, C, slab), bf(16, W), bf(16, W), bf(2, C, halo), bf(C, slab), bf(C, slab),
            bf(C, halo), bf(C, halo), bf(C, halo), bf(2, C, halo), bf(2, C, slab), bf(2, C, (H + 10) * W),
            bf(3 * C, 30 * W), bf(6 * C, halo), bf(3 * C, 26 * W), bf(2, 3 * C, 22 * W), bf(2, 3 * C, halo),
            f32(2, C, slab), f32(C, 24 * W), f32(C, halo), f32(C, 30 * W), f32(C, 24 * W),
            f32(2, C, halo), f32(2, C, (H + 4) * W), f32(C, 22 * W), f32(C, slab), f32(2, C, slab),
            bf(2, C, 7 * W), bf(2, C, 7 * W), bf(2, C, 4 * W), bf(2, C, 4 * W), bf(2, C, 3 * W), bf(2, C, 3 * W),
            bf(C, slab), bf(C, slab), bf(C, slab), bf(C, slab),
            bf(C, slab), bf(C, slab), bf(C, slab), bf(C, slab), bf(C, slab),
            bf(2, 5, 3 * C, 3 * C), bf(2, 4, 3 * C, 3 * C), bf(2, 3 * C, 6 * C), bf(2, 6 * C, 3 * C),
            pltpu.SemaphoreType.DMA((28,)), pltpu.SemaphoreType.DMA((28,)),
        ]

        def kernel(*refs):
            body(nt, ns, *refs)

        out, rg = pl.pallas_call(
            kernel,
            out_shape=(
                jax.ShapeDtypeStruct((2, C, slab), BF),
                jax.ShapeDtypeStruct((2, C, slab), F32),
            ),
            in_specs=[pl.BlockSpec(memory_space=pltpu.SMEM)] + [vmem] * 5,
            out_specs=(vmem, vmem),
            scratch_shapes=scratch,
            compiler_params=pltpu.CompilerParams(
                collective_id=0, has_side_effects=True, vmem_limit_bytes=56 << 20
            ),
            name="coding",
        )(level_table, current, contexts, cotangent, w_first, w_rest)
        return out.reshape(2, C, H, W), rg.reshape(2, C, H, W)

    frames = P("tm", None, "space", None)
    return jax.shard_map(
        on_device,
        mesh=mesh,
        in_specs=(frames, frames, frames, P("tm"), P("tm", None), P(), P()),
        out_specs=(frames, frames),
        check_vma=False,
    )
```

time: 67.9 us -> 62.1 us (0.915)
  the two profiles are of different devices: /device:TPU:169 before, /device:TPU:97 now
where the time goes in v1:
time: 62.1 us; the launch traced here: 62 us
  Pallas kernels  58.2 us (94%)
  local copies, waits for them, and re-layouts  3.2 us (5%)
  between operations  0.65 us (1%)
    pallas_call x1, Pallas kernels, on_device(): pl.pallas_call(kernel, out_shape=(jax.ShapeDtypeStruct((2, C, slab), BF),...  58.2 us
    unnamed x4, local copies, waits for them, and re-layouts  3.2 us

profile of v1, /device:TPU:97, one launch (start us, length us, event | category | flops | bytes accessed | tf_op | source)
XLA Modules:
  0.0 62.0 jit_solution(9309978134155055420)
XLA Ops:
  0.6 58.2 %coding.1 = (bf16[2,64,2048]{2,1,0:T(8,128)(2,1)}, f32[2,64,2048]{2,1,0:T(8,128)}) custom-call(s32[2]{0:T(128)} %refs_0_.1, bf16[2,64,16,128]{3,2,1,0:T(8,128)(2,1)} %refs_1_.1, bf16[2,64,16,128]{3,2,1,0:T(8,128)(2,1)} %refs_2_.1, bf16[2,64,16,128]{3,2,1,0:T(8,128)(2,1)} %refs_3_.1, bf16[2,9,64,192]{3,2,1,0:T(8,128)(2,1)} %refs_4_.1, ...), custom_call_target="tpu_custom_call" | custom-call | tf_op jit(solution)/shard_map/coding/pallas_call | solution.py:378
  58.8 0.0 copy-start
  58.8 2.0 %copy.8 = bf16[16,8,16,128]{3,2,1,0:T(8,128)(2,1)} copy(bf16[16,8,16,128]{3,1,2,0:T(8,128)(2,1)} %bitcast.11) | data formatting | bytes 1048576
  60.8 0.0 copy-done
  60.8 1.2 %copy.9 = f32[16,8,16,128]{3,2,1,0:T(8,128)} copy(f32[16,8,16,128]{3,1,2,0:T(8,128)S(1)} %bitcast.9) | data formatting | bytes 2097152
Async XLA Ops:
  58.8 2.0 %copy-start = (f32[2,64,2048]{2,1,0:T(8,128)S(1)}, f32[2,64,2048]{2,1,0:T(8,128)}, u32[]{:S(2)}) copy-start(f32[2,64,2048]{2,1,0:T(8,128)} %get-tuple-element.5) | copy-start | bytes 3145732

commit v2 on v1

--- a/solution.py
+++ b/solution.py
@@ -43,11 +43,12 @@
 
 
 def body(
-    nt, ns, level, cur, ctx, cot, wf, wr, out, rg,
+    nt, ns, level, cur_in, ctx_in, cot_in, wf_in, wr_in, out, rg,
+    cur, ctx, cot, wf, wr,
     flat, tctx, flag_s, flag_r, mctx, sel_o, sel_l, x_o, x_l, m_l, tcur, tcot, ccot,
     stack, stack_c, stack_g, stack_3, stack_4, p1_cur, g4_o, g4_e, p1_o, p1_e, d1, d2, d3_o, d3_e, outs,
     h1o_s, h1o_r, h1e_s, h1e_r, h3_s, h3_r, om_s, om_r, ox_s, ox_r, em_s, em_r, ex_s, ex_r, ey_r,
-    w_fwd, w_bwd, w_ctx, w_back, ssem, rsem,
+    w_fwd, w_bwd, w_ctx, w_back, ssem, rsem, lsem,
 ):
     tm = lax.axis_index("tm")
     sp = lax.axis_index("space")
@@ -105,6 +106,13 @@
         def _():
             pl.semaphore_signal(barrier, inc=1, device_id=(a, b), device_id_type=MESH)
 
+    loads = [
+        pltpu.make_async_copy(src, dst, lsem.at[i])
+        for i, (src, dst) in enumerate(((ctx_in, ctx), (cur_in, cur), (cot_in, cot), (wf_in, wf), (wr_in, wr)))
+    ]
+    for load in loads:
+        load.start()
+
     def rows_first(src, i, dst, row0):
         flat[...] = src[i].astype(F32).reshape(C * H, W)
         for r in range(H):
@@ -114,6 +122,7 @@
     has_l1 = level[1] == 1
     has_l = has_l0 | has_l1
     flag_s[...] = jnp.full((16, W), jnp.where(has_l0, 1.0, 0.0), F32).astype(BF)
+    loads[0].wait()
     for i in range(2):
         rows_first(ctx, i, tctx, 0)
     spans = 1 + up_ok.astype(jnp.int32) + dn_ok.astype(jnp.int32)
@@ -123,6 +132,7 @@
     send(1, tctx, mctx.at[:, :, lanes(1, H)], (mate, sp), always, always)
     send(2, tctx.at[:, :, lanes(H - 1, 1)], mctx.at[:, :, lanes(0, 1)], (mate, sp + 1), up_ok, dn_ok)
     send(3, tctx.at[:, :, lanes(0, 1)], mctx.at[:, :, lanes(H + 1, 1)], (mate, sp - 1), dn_ok, up_ok)
+    loads[1].wait()
     for i in range(2):
         rows_first(cur, i, tcur, 1)
     send(4, tcur.at[:, :, lanes(H, 1)], tcur.at[:, :, lanes(0, 1)], (tm, sp + 1), up_ok, dn_ok)
@@ -148,6 +158,7 @@
     send(11, sel_l.at[:, lanes(0, 1)], x_l.at[:, lanes(H + 1, 1)], (cross, sp - 1), cross_ok & dn_ok, cross_ok & up_ok)
     sel_o[...] = pick(ODD, tctx[0], tctx[1]).astype(BF)
 
+    loads[2].wait()
     for i in range(2):
         rows_first(cot, i, tcot, 0)
     for c, halo in ((ODD, 5), (EVEN, 2)):
@@ -184,6 +195,8 @@
     clear(cross_ok, ex_r, lanes(0, H), 1)
     clear(mate_cross_ok, ey_r, lanes(0, H), 1)
 
+    loads[3].wait()
+    loads[4].wait()
     eye_r = lax.broadcasted_iota(jnp.int32, (3 * C, 3 * C), 0)
     eye_c = lax.broadcasted_iota(jnp.int32, (3 * C, 3 * C), 1)
     eye = jnp.where(eye_r == eye_c, 1.0, 0.0).astype(BF)
@@ -312,9 +325,9 @@
     arrive(22)
     inner = jnp.where(has_l, m_l[...].astype(F32), pick(EVEN, mctx[0], mctx[1]))
     layer_one(EVEN, x_l[...].astype(F32), inner)
-    forward(EVEN)
     arrive(6, 7, 8)
     layer_one(ODD, x_o[...].astype(F32), pick(ODD, mctx[0], mctx[1]))
+    forward(EVEN)
     outer_g, inner_g = backward(EVEN)
     em_s[...] = inner_g.astype(BF)
     send(25, em_s, em_r, (mate, sp), always, always)
@@ -331,8 +344,14 @@
     send(24, om_s, om_r, (mate, sp), always, always)
     finish(ODD)
     mask = wide(H)
-    out[0] = jnp.where(mask, outs[EVEN], outs[ODD]).astype(BF)
-    out[1] = jnp.where(mask, outs[ODD], outs[EVEN]).astype(BF)
+
+    def channels_first(dst, i, value):
+        for r in range(H):
+            flat[pl.ds(r, C, stride=H), :] = value[:, lanes(r, 1)]
+        dst[i] = flat[...].reshape(C, H, W).astype(dst.dtype)
+
+    channels_first(out, 0, jnp.where(mask, outs[EVEN], outs[ODD]))
+    channels_first(out, 1, jnp.where(mask, outs[ODD], outs[EVEN]))
     arrive(26)
     send(27, ex_r, ey_r, (mate, sp), cross_ok, mate_cross_ok)
     arrive(27)
@@ -340,8 +359,8 @@
     even_g = jnp.where(has_l, even_g, 0.0)
     arrive(24, 23)
     odd_g = ox_r[...].astype(F32) + om_r[...].astype(F32)
-    rg[0] = jnp.where(mask, even_g, odd_g)
-    rg[1] = jnp.where(mask, odd_g, even_g)
+    channels_first(rg, 0, jnp.where(mask, even_g, odd_g))
+    channels_first(rg, 1, jnp.where(mask, odd_g, even_g))
     gone(*(i for i in sent if i not in left))
 
 
@@ -360,6 +379,7 @@
         slab = H * W
         halo = (H + 2) * W
         scratch = [
+            bf(2, C, H, W), bf(2, C, H, W), bf(2, C, H, W), bf(2, 9, C, 3 * C), bf(2, 4, 9, C, C),
             f32(C * H, W), bf(2, C, slab), bf(16, W), bf(16, W), bf(2, C, halo), bf(C, slab), bf(C, slab),
             bf(C, halo), bf(C, halo), bf(C, halo), bf(2, C, halo), bf(2, C, slab), bf(2, C, (H + 10) * W),
             bf(3 * C, 30 * W), bf(6 * C, halo), bf(3 * C, 26 * W), bf(2, 3 * C, 22 * W), bf(2, 3 * C, halo),
@@ -369,19 +389,19 @@
             bf(C, slab), bf(C, slab), bf(C, slab), bf(C, slab),
             bf(C, slab), bf(C, slab), bf(C, slab), bf(C, slab), bf(C, slab),
             bf(2, 5, 3 * C, 3 * C), bf(2, 4, 3 * C, 3 * C), bf(2, 3 * C, 6 * C), bf(2, 6 * C, 3 * C),
-            pltpu.SemaphoreType.DMA((28,)), pltpu.SemaphoreType.DMA((28,)),
+            pltpu.SemaphoreType.DMA((29,)), pltpu.SemaphoreType.DMA((29,)), pltpu.SemaphoreType.DMA((5,)),
         ]
 
         def kernel(*refs):
             body(nt, ns, *refs)
 
-        out, rg = pl.pallas_call(
+        return pl.pallas_call(
             kernel,
             out_shape=(
-                jax.ShapeDtypeStruct((2, C, slab), BF),
-                jax.ShapeDtypeStruct((2, C, slab), F32),
+                jax.ShapeDtypeStruct((2, C, H, W), BF),
+                jax.ShapeDtypeStruct((2, C, H, W), F32),
             ),
-            in_specs=[pl.BlockSpec(memory_space=pltpu.SMEM)] + [vmem] * 5,
+            in_specs=[pl.BlockSpec(memory_space=pltpu.SMEM)] + [pl.BlockSpec(memory_space=pl.ANY)] * 5,
             out_specs=(vmem, vmem),
             scratch_shapes=scratch,
             compiler_params=pltpu.CompilerParams(
@@ -389,7 +409,6 @@
             ),
             name="coding",
         )(level_table, current, contexts, cotangent, w_first, w_rest)
-        return out.reshape(2, C, H, W), rg.reshape(2, C, H, W)
 
     frames = P("tm", None, "space", None)
     return jax.shard_map(

time: 62.1 us -> 60.7 us (0.977)
  the two profiles are of different devices: /device:TPU:97 before, /device:TPU:67 now
where the time goes in v2:
time: 60.7 us; the launch traced here: 60.6 us
  Pallas kernels  57 us (94%)
  local copies, waits for them, and re-layouts  2.93 us (5%)
  between operations  0.65 us (1%)
    pallas_call x1, Pallas kernels, on_device(): pl.pallas_call(kernel, out_shape=(jax.ShapeDtypeStruct((2, C, H, W), BF),...  57 us
    unnamed x4, local copies, waits for them, and re-layouts  2.93 us

profile of v2, /device:TPU:67, one launch (start us, length us, event | category | flops | bytes accessed | tf_op | source)
XLA Modules:
  0.0 60.6 jit_solution(9142513847585424406)
XLA Ops:
  0.6 57.0 %coding.1 = (bf16[2,64,16,128]{3,2,1,0:T(8,128)(2,1)}, f32[2,64,16,128]{3,2,1,0:T(8,128)}) custom-call(s32[2]{0:T(128)} %refs_0_.1, bf16[2,64,16,128]{3,2,1,0:T(8,128)(2,1)} %refs_1_.1, bf16[2,64,16,128]{3,2,1,0:T(8,128)(2,1)} %refs_2_.1, bf16[2,64,16,128]{3,2,1,0:T(8,128)(2,1)} %refs_3_.1, bf16[2,9,64,192]{3,2,1,0:T(8,128)(2,1)} %refs_4_.1, ...), custom_call_target="tpu_custom_call" | custom-call | tf_op jit(solution)/shard_map/coding/pallas_call | solution.py:398
  57.6 0.0 copy-start
  57.6 2.0 %copy.10 = bf16[2,64,16,128]{3,2,1,0:T(8,128)(2,1)} copy(bf16[2,64,16,128]{3,2,1,0:T(8,128)(2,1)} %get-tuple-element.4) | data formatting | bytes 1048576
  59.6 0.0 copy-done
  59.6 1.0 %copy.11 = f32[2,64,16,128]{3,2,1,0:T(8,128)} copy(f32[2,64,16,128]{3,2,1,0:T(8,128)S(1)} %copy-done) | data formatting | bytes 2097152
Async XLA Ops:
  57.6 2.0 %copy-start = (f32[2,64,16,128]{3,2,1,0:T(8,128)S(1)}, f32[2,64,16,128]{3,2,1,0:T(8,128)}, u32[]{:S(2)}) copy-start(f32[2,64,16,128]{3,2,1,0:T(8,128)} %get-tuple-element.5) | copy-start | bytes 3145732

commit v3 on v2

--- a/solution.py
+++ b/solution.py
@@ -395,10 +395,10 @@
         def kernel(*refs):
             body(nt, ns, *refs)
 
-        return pl.pallas_call(
+        out, rg = pl.pallas_call(
             kernel,
             out_shape=(
-                jax.ShapeDtypeStruct((2, C, H, W), BF),
+                jax.ShapeDtypeStruct((2, C, H, W), F32),
                 jax.ShapeDtypeStruct((2, C, H, W), F32),
             ),
             in_specs=[pl.BlockSpec(memory_space=pltpu.SMEM)] + [pl.BlockSpec(memory_space=pl.ANY)] * 5,
@@ -409,6 +409,7 @@
             ),
             name="coding",
         )(level_table, current, contexts, cotangent, w_first, w_rest)
+        return out.astype(BF), rg
 
     frames = P("tm", None, "space", None)
     return jax.shard_map(

time: 60.7 us -> 61.1 us (level)
  other arithmetic: 0 us -> 2.17 us
  local copies, waits for them, and re-layouts: 2.93 us -> 0.97 us
    convert_element_type x0 -> x1, other arithmetic: none -> 2.17 us  [on_device(): return (out.astype(BF), rg)]
    unnamed x4 -> x3, local copies, waits for them, and re-layouts: 2.93 us -> 0.97 us
where the time goes in v3:
time: 61.1 us; the launch traced here: 60.9 us
  Pallas kernels  57.1 us (93%)
  other arithmetic  2.17 us (4%)
  local copies, waits for them, and re-layouts  0.97 us (2%)
  between operations  0.65 us (1%)
    pallas_call x1, Pallas kernels, on_device(): pl.pallas_call(kernel, out_shape=(jax.ShapeDtypeStruct((2, C, H, W), F32)...  57.1 us
    convert_element_type x1, other arithmetic, on_device(): return (out.astype(BF), rg)  2.17 us

profile of v3, /device:TPU:67, one launch (start us, length us, event | category | flops | bytes accessed | tf_op | source)
XLA Modules:
  0.0 60.9 jit_solution(2058646322336172924)
XLA Ops:
  0.6 57.1 %coding.1 = (f32[2,64,16,128]{3,2,1,0:T(8,128)}, f32[2,64,16,128]{3,2,1,0:T(8,128)}) custom-call(s32[2]{0:T(128)} %refs_0_.1, bf16[2,64,16,128]{3,2,1,0:T(8,128)(2,1)} %refs_1_.1, bf16[2,64,16,128]{3,2,1,0:T(8,128)(2,1)} %refs_2_.1, bf16[2,64,16,128]{3,2,1,0:T(8,128)(2,1)} %refs_3_.1, bf16[2,9,64,192]{3,2,1,0:T(8,128)(2,1)} %refs_4_.1, ...), custom_call_target="tpu_custom_call" | custom-call | tf_op jit(solution)/shard_map/coding/pallas_call | solution.py:398
  57.8 0.0 copy-start
  57.8 2.2 %convert_element_type.3 = bf16[2,64,16,128]{3,2,1,0:T(8,128)(2,1)} convert(f32[2,64,16,128]{3,2,1,0:T(8,128)} %get-tuple-element.4) | non-fusion elementwise | flops 262144 | bytes 1572864 | tf_op jit(solution)/shard_map/convert_element_type | solution.py:412
  60.0 0.0 copy-done
  60.0 1.0 %copy.9 = f32[2,64,16,128]{3,2,1,0:T(8,128)} copy(f32[2,64,16,128]{3,2,1,0:T(8,128)S(1)} %copy-done) | data formatting | bytes 2097152
Async XLA Ops:
  57.8 2.2 %copy-start = (f32[2,64,16,128]{3,2,1,0:T(8,128)S(1)}, f32[2,64,16,128]{3,2,1,0:T(8,128)}, u32[]{:S(2)}) copy-start(f32[2,64,16,128]{3,2,1,0:T(8,128)} %get-tuple-element.9) | copy-start | bytes 3145732
